TPU v7x, 128 devices: a whole 4x4x4 slice. The times are simulated.
128 devices in a mesh: blk: 8 (over x_lo, y), grp: 16 (over z, x_hi, core).
Axes of the slice: x: 4 (x_hi: 2, x_lo: 2; x = x_hi * 2 + x_lo), y: 4, z: 4, core: 2. Of those that a mesh axis runs over, the one named last changes fastest.
Arguments:
- picture_vectors: bfloat16 [16384, 1152], P(('blk', 'grp')), may hold values from -1.1953125 to 1.1953125
- caption_vectors: bfloat16 [16384, 1152], P(('blk', 'grp')), may hold values from -1.1953125 to 1.1953125
- matching_caption: int32 [16384], P(('blk', 'grp')), may hold values from 0 to 16383, each once
- sharpness_parameter: float32 [1], replicated, may hold values from 1 to 4
- additive_intercept: float32 [1], replicated, may hold values from -6 to -2
Outputs:
- picture_derivative: float32 [16384, 1152], P(('blk', 'grp'))
- text_grad: float32 [16384, 1152], P(('blk', 'grp'))
Inputs may be any that keep to these rules, and one draw needn't show every extreme that they name: matching_caption is a permutation: each text is the positive of exactly one image.
All inputs are finite; a program needn't handle non-finite values.
Results may differ from a plain program's by a relative error of at most 0.0011.
Values may be sent and summed in bfloat16 or wider, within the bound.
A program may use at most 64 MiB of HBM per device.

v0:
```python
import jax
import jax.numpy as jnp
from jax import lax
from jax.sharding import PartitionSpec as P


def passed_along(block, axis, distance):
    devices = range(lax.axis_size(axis))
    route = [((i - distance) % len(devices), i) for i in devices]
    return lax.ppermute(block, axis, route)


def rotation_step(
    cohort_pictures,
    cohort_labels,
    guest_captions,
    caption_numbers,
    sharpness_factor,
    moved_intercept,
):
    similarity_matrix = lax.dot_general(
        cohort_pictures,
        guest_captions,
        (((1,), (1,)), ((), ())),
        preferred_element_type=jnp.float32,
    )
    matching_pair = (cohort_labels[:, None] == caption_numbers[None, :]).astype(jnp.float32)
    pair_coefficients = (
        jax.nn.sigmoid(sharpness_factor * similarity_matrix + moved_intercept) - matching_pair
    ).astype(jnp.bfloat16)
    image_part = jnp.dot(pair_coefficients, guest_captions, preferred_element_type=jnp.float32)
    partial_value = lax.dot_general(
        pair_coefficients,
        cohort_pictures,
        (((0,), (0,)), ((), ())),
        preferred_element_type=jnp.float32,
    )
    return (image_part, partial_value)


def per_device(
    picture_vectors, caption_vectors, matching_caption, sharpness_parameter, additive_intercept
):
    sharpness_factor = sharpness_parameter[0]
    moved_intercept = additive_intercept[0]
    local_count = picture_vectors.shape[0]
    width = picture_vectors.shape[1]
    block_total = lax.axis_size("blk")
    grp_count = lax.axis_size("grp")
    current_block = lax.axis_index("blk")
    current_group = lax.axis_index("grp")
    local_ids = jnp.arange(local_count, dtype=jnp.int32)
    cohort_pictures, cohort_labels = (
        lax.all_gather(picture_vectors, "grp", axis=0, tiled=True),
        lax.all_gather(matching_caption, "grp", axis=0, tiled=True),
    )
    image_total = jnp.zeros((cohort_pictures.shape[0], width), jnp.float32)
    holding_buffer = jnp.zeros((block_total, local_count, width), jnp.float32)
    guest_captions = caption_vectors
    for turn in range(block_total):
        source = (current_block - turn + block_total) % block_total
        caption_numbers = (source * grp_count + current_group) * local_count + local_ids
        image_part, partial_value = rotation_step(
            cohort_pictures,
            cohort_labels,
            guest_captions,
            caption_numbers,
            sharpness_factor,
            moved_intercept,
        )
        image_total = image_total + image_part
        holding_buffer = lax.dynamic_update_index_in_dim(holding_buffer, partial_value, source, 0)
        if turn + 1 < block_total:
            guest_captions = passed_along(guest_captions, "blk", 1)
    picture_derivative = sharpness_factor * lax.psum_scatter(
        image_total, "grp", scatter_dimension=0, tiled=True
    )
    text_grad = (
        sharpness_factor
        * lax.psum_scatter(holding_buffer, "blk", scatter_dimension=0, tiled=True)[0]
    )
    return (picture_derivative, text_grad)


def solution(mesh):
    placed = (P(("blk", "grp"), None), P(("blk", "grp"), None), P(("blk", "grp")), P(), P())
    return jax.shard_map(
        per_device,
        mesh=mesh,
        in_specs=placed,
        out_specs=(P(("blk", "grp"), None), P(("blk", "grp"), None)),
        check_vma=False,
    )
```

profile of v0, /device:TPU:1, one launch (start us, length us, event | category | flops | bytes accessed | tf_op | source)
XLA Modules:
  0.0 301.0 jit_solution(14475134431109681809)
XLA Ops:
  7.9 2.2 collective-permute-start
  10.1 9.2 %collective-permute-done = bf16[128,1152]{1,0:T(8,128)(2,1)S(1)} collective-permute-done((bf16[128,1152]{1,0:T(8,128)(2,1)}, bf16[128,1152]{1,0:T(8,128)(2,1)S(1)}, u32[]{:S(2)}, u32[]{:S(2)}) %collective-permute-start) | collective-permute-done | bytes 294944 | tf_op jit(solution)/shard_map/ppermute | solution.py:10
  19.3 9.4 %collective-permute-done.1 = bf16[128,1152]{1,0:T(8,128)(2,1)S(1)} collective-permute-done((bf16[128,1152]{1,0:T(8,128)(2,1)S(1)}, bf16[128,1152]{1,0:T(8,128)(2,1)S(1)}, u32[]{:S(2)}, u32[]{:S(2)}) %collective-permute-start.1) | collective-permute-done | bytes 294944 | tf_op jit(solution)/shard_map/ppermute | solution.py:10
  28.7 7.8 %collective-permute-done.2 = bf16[128,1152]{1,0:T(8,128)(2,1)S(1)} collective-permute-done((bf16[128,1152]{1,0:T(8,128)(2,1)S(1)}, bf16[128,1152]{1,0:T(8,128)(2,1)S(1)}, u32[]{:S(2)}, u32[]{:S(2)}) %collective-permute-start.2) | collective-permute-done | bytes 294944 | tf_op jit(solution)/shard_map/ppermute | solution.py:10
  37.9 32.2 %all-gather = s32[16,1,128]{2,1,0:T(1,128)S(1)} all-gather(s32[1,1,128]{2,1,0:T(1,128)} %bitcast.112), channel_id=1, replica_groups=mesh['blk'=8,'grp'=16] {'grp'}, dimensions={0}, use_global_device_ids=true | all-gather | bytes 8704 | tf_op jit(solution)/shard_map/all_gather | solution.py:55
  70.2 10.5 %collective-permute-done.4 = bf16[128,1152]{1,0:T(8,128)(2,1)S(1)} collective-permute-done((bf16[128,1152]{1,0:T(8,128)(2,1)S(1)}, bf16[128,1152]{1,0:T(8,128)(2,1)S(1)}, u32[]{:S(2)}, u32[]{:S(2)}) %collective-permute-start.4) | collective-permute-done | bytes 294944 | tf_op jit(solution)/shard_map/ppermute | solution.py:10
  80.7 9.7 %collective-permute-done.5 = bf16[128,1152]{1,0:T(8,128)(2,1)} collective-permute-done((bf16[128,1152]{1,0:T(8,128)(2,1)S(1)}, bf16[128,1152]{1,0:T(8,128)(2,1)}, u32[]{:S(2)}, u32[]{:S(2)}) %collective-permute-start.5) | collective-permute-done | bytes 294944 | tf_op jit(solution)/shard_map/ppermute | solution.py:10
  90.4 4.0 %fusion.56 = bf16[2048,128]{1,0:T(8,128)(2,1)S(1)} fusion(bf16[2048,1152]{1,0:T(8,128)(2,1)} %all-gather.3.cloned.1.call-done, bf16[128,1152]{1,0:T(8,128)(2,1)} %param.6, s32[128]{0:T(128)S(1)} %iota_add_fusion.7, f32[]{:T(128)} %bitcast.96, f32[]{:T(128)} %bitcast.87, s32[2048]{0:T(1024)S(1)} %bitcast.104), kind=kOutput, calls=%fused_computation.79 | convolution fusion | flops 606339072 | bytes 5546504 | tf_op jit(solution)/shard_map/dot_general | solution.py:21
  94.5 1.9 fusion.57
  96.4 1.7 fusion.58
  98.1 1.7 fusion.59
  99.9 1.7 fusion.60
  101.6 1.7 fusion.61
  103.3 2.7 fusion.62
  106.0 2.6 broadcast_in_dim.44
  108.7 1.7 fusion.7
  110.4 1.7 fusion.6
  112.1 1.7 fusion.5
  113.8 1.8 fusion.4
  115.6 1.7 fusion.3
  117.3 1.7 fusion.2
  119.0 1.7 fusion.1
  120.7 2.7 fusion.63
  124.2 1.7 fusion
  129.0 1.4 convolution_add_fusion.5
  133.3 1.4 convolution_add_fusion.2
  134.8 2.4 convolution_add_fusion.1
  137.2 6.0 %convolution_add_fusion = f32[2048,1152]{1,0:T(8,128)} fusion(f32[2048,1152]{1,0:T(8,128)S(1)} %convolution_add_fusion.1, bf16[2048,128]{1,0:T(8,128)(2,1)S(1)} %copy-done.4, bf16[128,1152]{1,0:T(8,128)(2,1)} %collective-permute-done.6), kind=kOutput, calls=%fused_computation | convolution fusion | flops 606339072 | bytes 19693568 | tf_op jit(solution)/shard_map/dot_general | solution.py:31
  143.2 39.7 %reduce-scatter.5.cloned.1.call-done = f32[1,128,1152]{2,1,0:T(8,128)} async-done(((f32[8,128,1152]{2,1,0:T(8,128)}), f32[1,128,1152]{2,1,0:T(8,128)}) %reduce-scatter.5.cloned.1.call-update) | async-done | bytes 589840 | tf_op jit(solution)/shard_map/reduce_scatter | solution.py:80
  183.0 1.9 multiply_bitcast_fusion
  184.9 107.7 %reduce-scatter.3.cloned.1.call-done = f32[128,1152]{1,0:T(8,128)} async-done(((f32[2048,1152]{1,0:T(8,128)}), f32[128,1152]{1,0:T(8,128)}) %reduce-scatter.3.cloned.1.call-update) | async-done | bytes 589840 | tf_op jit(solution)/shard_map/reduce_scatter | solution.py:75
  292.6 1.9 broadcast_multiply_fusion
  (61 shorter events, 7.6 us)
Async XLA Ops:
  7.2 83.2 %all-gather.3.cloned.1.call-start = ((), (), s32[]{:S(2)}) async-start(), calls=%async_computation.2 | async-start | bytes 5013504 | tf_op jit(solution)/shard_map/all_gather | solution.py:54
  7.9 175.1 %reduce-scatter.5.cloned.1.call-start = ((), (), s32[]{:S(2)}) async-start(), calls=%async_computation.4 | async-start | bytes 5308416 | tf_op jit(solution)/shard_map/reduce_scatter | solution.py:80
  7.9 11.4 %collective-permute-start = (bf16[128,1152]{1,0:T(8,128)(2,1)}, bf16[128,1152]{1,0:T(8,128)(2,1)S(1)}, u32[]{:S(2)}, u32[]{:S(2)}) collective-permute-start(bf16[128,1152]{1,0:T(8,128)(2,1)} %param.6), channel_id=1, source_target_pairs={{112,0},{0,16},{16,32},{32,48},{48,64},{64,80},{80,96},{96,112},{1... | collective-permute-start | bytes 884744 | tf_op jit(solution)/shard_map/ppermute | solution.py:10
  19.3 75.1 %copy-start.6 = (bf16[128,1152]{1,0:T(8,128)(2,1)}, bf16[128,1152]{1,0:T(8,128)(2,1)S(1)}, u32[]{:S(2)}) copy-start(bf16[128,1152]{1,0:T(8,128)(2,1)S(1)} %collective-permute-done) | copy-start | bytes 884740
  19.3 9.4 %collective-permute-start.1 = (bf16[128,1152]{1,0:T(8,128)(2,1)S(1)}, bf16[128,1152]{1,0:T(8,128)(2,1)S(1)}, u32[]{:S(2)}, u32[]{:S(2)}) collective-permute-start(bf16[128,1152]{1,0:T(8,128)(2,1)S(1)} %collective-permute-done), channel_id=1, source_target_pairs={{112,0},{0,16},{16,32},{32,48},{48,64},{64,80},{80,96},{96,112},{1... | collective-permute-start | bytes 884744 | tf_op jit(solution)/shard_map/ppermute | solution.py:10
  28.7 67.7 %copy-start.8 = (bf16[128,1152]{1,0:T(8,128)(2,1)}, bf16[128,1152]{1,0:T(8,128)(2,1)S(1)}, u32[]{:S(2)}) copy-start(bf16[128,1152]{1,0:T(8,128)(2,1)S(1)} %collective-permute-done.1) | copy-start | bytes 884740
  28.7 7.8 %collective-permute-start.2 = (bf16[128,1152]{1,0:T(8,128)(2,1)S(1)}, bf16[128,1152]{1,0:T(8,128)(2,1)S(1)}, u32[]{:S(2)}, u32[]{:S(2)}) collective-permute-start(bf16[128,1152]{1,0:T(8,128)(2,1)S(1)} %collective-permute-done.1), channel_id=1, source_target_pairs={{112,0},{0,16},{16,32},{32,48},{48,64},{64,80},{80,96},{96,112},{1... | collective-permute-start | bytes 884744 | tf_op jit(solution)/shard_map/ppermute | solution.py:10
  36.5 61.6 %copy-start.10 = (bf16[128,1152]{1,0:T(8,128)(2,1)}, bf16[128,1152]{1,0:T(8,128)(2,1)S(1)}, u32[]{:S(2)}) copy-start(bf16[128,1152]{1,0:T(8,128)(2,1)S(1)} %collective-permute-done.2) | copy-start | bytes 884740
  36.5 33.5 %collective-permute-start.3 = (bf16[128,1152]{1,0:T(8,128)(2,1)S(1)}, bf16[128,1152]{1,0:T(8,128)(2,1)S(1)}, u32[]{:S(2)}, u32[]{:S(2)}) collective-permute-start(bf16[128,1152]{1,0:T(8,128)(2,1)S(1)} %collective-permute-done.2), channel_id=1, source_target_pairs={{112,0},{0,16},{16,32},{32,48},{48,64},{64,80},{80,96},{96,112},{1... | collective-permute-start | bytes 884744 | tf_op jit(solution)/shard_map/ppermute | solution.py:10
  70.1 29.8 %copy-start.12 = (bf16[128,1152]{1,0:T(8,128)(2,1)}, bf16[128,1152]{1,0:T(8,128)(2,1)S(1)}, u32[]{:S(2)}) copy-start(bf16[128,1152]{1,0:T(8,128)(2,1)S(1)} %collective-permute-done.3) | copy-start | bytes 884740
  70.1 10.6 %collective-permute-start.4 = (bf16[128,1152]{1,0:T(8,128)(2,1)S(1)}, bf16[128,1152]{1,0:T(8,128)(2,1)S(1)}, u32[]{:S(2)}, u32[]{:S(2)}) collective-permute-start(bf16[128,1152]{1,0:T(8,128)(2,1)S(1)} %collective-permute-done.3), channel_id=1, source_target_pairs={{112,0},{0,16},{16,32},{32,48},{48,64},{64,80},{80,96},{96,112},{1... | collective-permute-start | bytes 884744 | tf_op jit(solution)/shard_map/ppermute | solution.py:10
  80.7 13.8 %copy-start.14 = (bf16[128,1152]{1,0:T(8,128)(2,1)}, bf16[128,1152]{1,0:T(8,128)(2,1)S(1)}, u32[]{:S(2)}) copy-start(bf16[128,1152]{1,0:T(8,128)(2,1)S(1)} %collective-permute-done.4) | copy-start | bytes 884740
  80.7 9.7 %collective-permute-start.5 = (bf16[128,1152]{1,0:T(8,128)(2,1)S(1)}, bf16[128,1152]{1,0:T(8,128)(2,1)}, u32[]{:S(2)}, u32[]{:S(2)}) collective-permute-start(bf16[128,1152]{1,0:T(8,128)(2,1)S(1)} %collective-permute-done.4), channel_id=1, source_target_pairs={{112,0},{0,16},{16,32},{32,48},{48,64},{64,80},{80,96},{96,112},{1... | collective-permute-start | bytes 884744 | tf_op jit(solution)/shard_map/ppermute | solution.py:10
  90.4 30.3 %collective-permute-start.6 = (bf16[128,1152]{1,0:T(8,128)(2,1)}, bf16[128,1152]{1,0:T(8,128)(2,1)}, u32[]{:S(2)}, u32[]{:S(2)}) collective-permute-start(bf16[128,1152]{1,0:T(8,128)(2,1)} %collective-permute-done.5), channel_id=1, source_target_pairs={{112,0},{0,16},{16,32},{32,48},{48,64},{64,80},{80,96},{96,112},{1... | collective-permute-start | bytes 884744 | tf_op jit(solution)/shard_map/ppermute | solution.py:10
  90.4 4.1 %copy-start = (bf16[2048,1152]{1,0:T(8,128)(2,1)S(1)}, bf16[2048,1152]{1,0:T(8,128)(2,1)}, u32[]{:S(2)}) copy-start(bf16[2048,1152]{1,0:T(8,128)(2,1)} %all-gather.3.cloned.1.call-done) | copy-start | bytes 14155780
  96.4 14.0 %copy-start.1 = (bf16[2048,128]{1,0:T(8,128)(2,1)}, bf16[2048,128]{1,0:T(8,128)(2,1)S(1)}, u32[]{:S(2)}) copy-start(bf16[2048,128]{1,0:T(8,128)(2,1)S(1)} %fusion.57) | copy-start | bytes 1572868
  99.9 1.7 copy-start.15
  123.4 0.8 copy-start.3
  124.2 2.0 copy-start.5
  125.9 166.6 %reduce-scatter.3.cloned.1.call-start = ((), (), s32[]{:S(2)}) async-start(), calls=%async_computation.3 | async-start | bytes 10027008 | tf_op jit(solution)/shard_map/reduce_scatter | solution.py:75
  126.2 1.4 copy-start.2
  126.2 1.4 copy-start.7
  127.6 1.4 copy-start.9
  129.0 1.4 copy-start.11
  130.5 1.4 copy-start.13
  131.9 1.4 copy-start.16
  134.7 2.4 copy-start.4
Sparse Core Ops, SparseCore 0:
  10.5 62.9 all-gather.2
  126.1 56.8 reduce-scatter.4
  187.3 105.2 reduce-scatter.2
where the time goes:
time: 301 us
  waiting for transfers between devices  195 us (65%)
  matrix products  48.8 us (16%)
  blocking collectives  32.2 us (11%)
  between operations  15.4 us (5%)
  other arithmetic  3.88 us (1%)
  local copies, waits for them, and re-layouts  3.46 us (1%)
    reduce_scatter x1, waiting for transfers between devices, per_device(): lax.psum_scatter(image_total, 'grp', scatter_dimension=0, tiled=True)  108 us
    ppermute x7, waiting for transfers between devices, passed_along(): return lax.ppermute(block, axis, route)  46.5 us
    reduce_scatter x1, waiting for transfers between devices, per_device(): lax.psum_scatter(holding_buffer, 'blk', scatter_dimension=0, tiled=True)[0]  39.7 us
    all_gather x1, blocking collectives, per_device(): lax.all_gather(matching_caption, 'grp', axis=0, tiled=True)  32.2 us
    dot_general x8, matrix products, rotation_step(): lax.dot_general(cohort_pictures, guest_captions, (((1,), (1,)), ((), ()))...  18.2 us
    dot_general x8, matrix products, rotation_step(): jnp.dot(pair_coefficients, guest_captions, preferred_element_type=jnp.flo...  16.8 us
    dot_general x8, matrix products, rotation_step(): lax.dot_general(pair_coefficients, cohort_pictures, (((0,), (0,)), ((), (...  13.8 us
  transfers between devices with their start and end apart: 10, of which 7 were waited for; matrix products, arithmetic and copies ran while one was open for 16% of the time, Pallas kernels for 0%

commit v1 on v0

v1 whole, which is shorter than its diff:
```python
import functools

import jax
import jax.numpy as jnp
from jax import lax
from jax.experimental import pallas as pl
from jax.experimental.pallas import tpu as pltpu
from jax.sharding import PartitionSpec as P

MESH = pl.DeviceIdType.MESH
ORDER = [(0, 0), (3, 0), (1, 0), (2, 0), (0, 1), (3, 1), (1, 1), (2, 1)]
SLOT = {key: i for i, key in enumerate(ORDER)}
SHARE = 128
HALF = 64
UNIT = 32
MESSAGES = 17
TOP = 32767.0


def peers():
    b, g = lax.axis_index("blk"), lax.axis_index("grp")
    xl, y = b // 4, lax.rem(b, 4)
    z, low = g // 4, lax.rem(g, 4)
    xh, core = low // 2, lax.rem(low, 2)

    def at(xl, y, z, xh, core):
        return (xl * 4 + y, z * 4 + xh * 2 + core)

    up = lambda v: lax.rem(v + 1, 4)
    down = lambda v: lax.rem(v + 3, 4)
    pictures = (at(xl, y, up(z), xh, core), at(xl, y, down(z), xh, core), at(1 - xl, y, z, xh, core))
    captions = (at(xl, up(y), z, xh, core), at(xl, down(y), z, xh, core), at(1 - xl, y, z, 1 - xh, core))
    sibling = at(xl, y, z, xh, 1 - core)
    starts = []
    for dy, dx in ORDER:
        txl = 1 - xl if dx else xl
        txh = 1 - xh if dx else xh
        blk, grp = at(txl, lax.rem(y + dy, 4), z, txh, core)
        starts.append((blk * 16 + grp) * SHARE)
    return pictures, captions, sibling, starts


class Family:
    def __init__(self, shares, step, sums, other, devices, out, first):
        self.shares, self.step, self.sums, self.other = shares, step, sums, other
        self.plus, self.minus, self.pair = devices
        self.out, self.message = out, first
        self.sent = {}

    def rows(self, key, lo, hi):
        return self.shares.at[pl.ds(SLOT[key] * self.step + lo, hi - lo)]


def kernel(
    sharp_ref, shift_ref, picture_ref, caption_ref, label_ref, picture_out, caption_out,
    pictures, captions, labels, weights, picture_sums, caption_sums, sibling_sums,
    out_data, in_data, out_scale, in_scale, local_sem, send_sem, recv_sem,
):
    picture_peers, caption_peers, sibling, starts = peers()
    loads = [
        pltpu.make_async_copy(picture_ref, pictures.at[pl.ds(0, SHARE)], local_sem.at[0]),
        pltpu.make_async_copy(caption_ref, captions.at[pl.ds(0, SHARE)], local_sem.at[1]),
    ]
    for load in loads:
        load.start()
    barrier = pltpu.get_barrier_semaphore()
    everyone = [*picture_peers, *caption_peers, sibling]
    for device in everyone:
        pl.semaphore_signal(barrier, inc=1, device_id=device, device_id_type=MESH)
    labels[0] = jnp.broadcast_to(label_ref[...], (8, SHARE))
    half_sharp = sharp_ref[0] * 0.5
    half_shift = shift_ref[0] * 0.5
    for load in loads:
        load.wait()
    pl.semaphore_wait(barrier, len(everyone))

    copies = []

    def send(src, dst, device):
        i = len(copies)
        copy = pltpu.make_async_remote_copy(
            src_ref=src, dst_ref=dst, send_sem=send_sem.at[i], recv_sem=recv_sem.at[i],
            device_id=device, device_id_type=MESH,
        )
        copy.start()
        copies.append(copy)
        return copy

    images = Family(pictures, 2 * SHARE, picture_sums, sibling_sums, picture_peers, picture_out, 0)
    texts = Family(captions, SHARE, caption_sums, None, caption_peers, caption_out, MESSAGES)
    both = (images, texts)
    mid_p, mid_q = HALF // 2, HALF + HALF // 2

    def hop(f, name, key, lo, hi, to, device):
        f.sent[name] = send(f.rows(key, lo, hi), f.rows(to, lo, hi), device)

    def to_sibling(*keys):
        for key in keys:
            start = SLOT[key] * 2 * SHARE
            images.sent["s", key] = send(
                pictures.at[pl.ds(start, SHARE)], pictures.at[pl.ds(start + SHARE, SHARE)], sibling
            )

    def arrive(f, *names):
        for name in names:
            f.sent[name].wait_recv()

    for f in both:
        hop(f, "q+", (0, 0), HALF, SHARE, (3, 0), f.plus)
        hop(f, "q-", (0, 0), HALF, SHARE, (1, 0), f.minus)
        hop(f, "xp", (0, 0), 0, HALF, (0, 1), f.pair)
    to_sibling((0, 0))

    def label_copy(first, to, count, device):
        return send(labels.at[pl.ds(first, count)], labels.at[pl.ds(to, count)], device)

    label_copy(0, 1, 1, sibling).wait_recv()
    for f in both:
        hop(f, "p+", (0, 0), 0, HALF, (3, 0), f.plus)
        hop(f, "p-", (0, 0), 0, HALF, (1, 0), f.minus)
        hop(f, "xq", (0, 0), HALF, SHARE, (0, 1), f.pair)
    label_copy(0, 2 * SLOT[0, 1], 2, images.pair).wait_recv()
    rounds = []
    for dx in (0, 1):
        mine, above, below = (2 * SLOT[d, dx] for d in (0, 1, 3))
        rounds.append(label_copy(mine, below, 2, images.plus))
        rounds.append(label_copy(mine, above, 2, images.minus))
    for copy in rounds:
        copy.wait_recv()
    rounds = []
    for dx in (0, 1):
        below, across = 2 * SLOT[3, dx], 2 * SLOT[2, dx]
        rounds.append(label_copy(below, across, 2, images.plus))
    for copy in rounds:
        copy.wait_recv()

    for f in both:
        arrive(f, "q+", "q-")
        hop(f, "q++", (3, 0), HALF, mid_q, (2, 0), f.plus)
        hop(f, "q--", (1, 0), mid_q, SHARE, (2, 0), f.minus)
        hop(f, "xq1", (1, 0), HALF, SHARE, (1, 1), f.pair)
        hop(f, "xq3", (3, 0), HALF, SHARE, (3, 1), f.pair)
    for f in both:
        arrive(f, "xp")
        hop(f, "P+", (0, 1), 0, HALF, (3, 1), f.plus)
        hop(f, "P-", (0, 1), 0, HALF, (1, 1), f.minus)
    for f in both:
        arrive(f, "p+", "p-")
        hop(f, "p++", (3, 0), 0, mid_p, (2, 0), f.plus)
        hop(f, "p--", (1, 0), mid_p, HALF, (2, 0), f.minus)
    to_sibling((3, 0), (1, 0))
    for f in both:
        arrive(f, "q++", "q--")
        hop(f, "xq2", (2, 0), HALF, SHARE, (2, 1), f.pair)
    for f in both:
        arrive(f, "p++", "p--")
    to_sibling((2, 0))
    arrive(images, "xq")
    to_sibling((0, 1))
    arrive(texts, "xq")

    def weigh(first_text, first_image, count):
        @pl.loop(first_image, first_image + count)
        def _(ii):
            columns = pl.ds(pl.multiple_of(ii * 2 * SHARE, 2 * SHARE), 2 * SHARE)
            scores = lax.dot_general(
                captions[pl.ds(first_text * SHARE, 4 * SHARE), :], pictures[columns, :],
                (((1,), (1,)), ((), ())), preferred_element_type=jnp.float32,
            )
            label = jnp.concatenate([labels[2 * ii, :1, :], labels[2 * ii + 1, :1, :]], axis=1)
            ids = lax.broadcasted_iota(jnp.int32, (SHARE, 2 * SHARE), 0)
            for j in range(4):
                own = ids == label - starts[first_text + j]
                part = scores[j * SHARE : (j + 1) * SHARE] * half_sharp + half_shift
                twice = jnp.tanh(part) + jnp.where(own, -1.0, 1.0)
                weights[pl.ds((first_text + j) * SHARE, SHARE), columns] = twice.astype(jnp.bfloat16)

    arrive(images, ("s", (0, 0)), ("s", (3, 0)), ("s", (1, 0)), ("s", (2, 0)))
    weigh(0, 0, 4)
    for f in both:
        arrive(f, "P+", "P-")
        hop(f, "P++", (3, 1), 0, mid_p, (2, 1), f.plus)
        hop(f, "P--", (1, 1), mid_p, HALF, (2, 1), f.minus)
    arrive(images, "xq1", "xq3")
    to_sibling((3, 1), (1, 1))
    arrive(images, ("s", (0, 1)), ("s", (3, 1)), ("s", (1, 1)))
    weigh(0, 4, 3)
    arrive(images, "P++", "P--", "xq2")
    to_sibling((2, 1))
    arrive(texts, "xq1", "xq3", "P++", "P--", "xq2")
    weigh(4, 0, 7)
    arrive(images, ("s", (2, 1)))
    weigh(0, 7, 1)
    weigh(4, 7, 1)

    def multiply_pictures(key):
        rows = pl.ds(SLOT[key] * 2 * SHARE, 2 * SHARE)
        picture_sums[rows, :] = lax.dot_general(
            weights[:, rows], captions[...], (((0,), (0,)), ((), ())), preferred_element_type=jnp.float32
        )
        images.sent["t", key] = send(
            picture_sums.at[pl.ds(SLOT[key] * 2 * SHARE + SHARE, SHARE)], sibling_sums.at[SLOT[key]], sibling
        )

    def multiply_captions(key):
        rows = pl.ds(SLOT[key] * SHARE, SHARE)
        caption_sums[rows, :] = jnp.dot(weights[rows, :], pictures[...], preferred_element_type=jnp.float32)

    lanes = lax.broadcasted_iota(jnp.int32, (8, 128), 1)

    def unpacked(index, at):
        scale = in_scale[index]
        column = jnp.concatenate([scale[:, k : k + 1] for k in range(at // 8, (at + UNIT) // 8)], axis=0)
        return in_data[index, pl.ds(at, UNIT), :].astype(jnp.int32).astype(jnp.float32) * column

    def total(f, key, lo, arrived):
        x = f.sums[pl.ds(SLOT[key] * f.step + lo, UNIT), :]
        if f.other is not None:
            x = x + f.other[SLOT[key], pl.ds(lo, UNIT), :]
        for index, at in arrived:
            x = x + unpacked(index, at)
        return x

    def pass_on(f, name, key, lo, hi, arrived, device):
        index = f.message
        f.message += 1
        scale = jnp.zeros((8, 128), jnp.float32)
        for row in range(lo, hi, UNIT):
            x = total(f, key, row, arrived(row))
            peak = jnp.maximum(jnp.max(jnp.abs(x), axis=1, keepdims=True), 1e-30)
            whole = x * (TOP / peak)
            whole = (whole + 12582912.0) - 12582912.0
            out_data[index, pl.ds(row - lo, UNIT), :] = whole.astype(jnp.int32).astype(jnp.int16)
            for k in range(UNIT // 8):
                scale = jnp.where(lanes == (row - lo) // 8 + k, peak[8 * k : 8 * k + 8] * (1.0 / TOP), scale)
        out_scale[index] = scale
        span = pl.ds(0, hi - lo)
        data = send(out_data.at[index, span], in_data.at[index, span], device)
        f.sent[name] = (index, lo, hi, data, send(out_scale.at[index], in_scale.at[index], device))

    def landed(f, *names):
        for name in names:
            for copy in f.sent[name][3:]:
                copy.wait_recv()

    def came(f, *names):
        whole = [f.sent[name][:3] for name in names]
        return lambda row: [(i, row - lo) for i, lo, hi in whole if lo <= row < hi]

    def ring(f, d, dx, tag, lo, also=()):
        mid, hi = lo + HALF // 2, lo + HALF
        if d == 2:
            pass_on(f, tag + "a", (2, dx), lo, mid, came(f, *also), f.plus)
            pass_on(f, tag + "b", (2, dx), mid, hi, came(f, *also), f.minus)
        if d == 1:
            landed(f, tag + "a")
            pass_on(f, tag + "c", (1, dx), lo, hi, came(f, tag + "a", *also), f.plus)
        if d == 3:
            landed(f, tag + "b")
            pass_on(f, tag + "d", (3, dx), lo, hi, came(f, tag + "b", *also), f.minus)

    def reduce(f, key):
        d, dx = key
        if dx == 1:
            pass_on(f, f"x{d}", key, HALF, SHARE, came(f), f.pair)
            ring(f, d, 1, "P", 0)
            if d == 0:
                landed(f, "Pc", "Pd")
                pass_on(f, "xp'", key, 0, HALF, came(f, "Pc", "Pd"), f.pair)
            return
        ring(f, d, 0, "p", 0)
        landed(f, f"x{d}")
        ring(f, d, 0, "q", HALF, (f"x{d}",))
        if d == 0:
            landed(f, "pc", "pd", "qc", "qd", "xp'")
            for lo, names in ((0, ("pc", "pd", "xp'")), (HALF, ("x0", "qc", "qd"))):
                for row in range(lo, lo + HALF, UNIT):
                    f.out[pl.ds(row, UNIT), :] = total(f, key, row, came(f, *names)(row))

    for key in [(2, 1), (1, 1), (3, 1), (0, 1), (2, 0), (1, 0), (3, 0), (0, 0)]:
        multiply_pictures(key)
        multiply_captions(key)
        reduce(texts, key)
        arrive(images, ("t", key))
        reduce(images, key)
    for copy in copies:
        copy.wait_send()


COPIES = 34 + 8 + 8 + 8 + 4 * MESSAGES


def per_device(picture_vectors, caption_vectors, matching_caption, sharpness_parameter, additive_intercept):
    width = picture_vectors.shape[1]
    f32, bf16 = jnp.float32, jnp.bfloat16
    out = jax.ShapeDtypeStruct((SHARE, width), f32)
    vmem, smem = pl.BlockSpec(memory_space=pltpu.VMEM), pl.BlockSpec(memory_space=pltpu.SMEM)
    anywhere = pl.BlockSpec(memory_space=pl.ANY)
    picture_sums, caption_sums = pl.pallas_call(
        kernel,
        out_shape=(out, out),
        in_specs=[smem, smem, anywhere, anywhere, vmem],
        out_specs=(vmem, vmem),
        scratch_shapes=[
            pltpu.VMEM((16 * SHARE, width), bf16),
            pltpu.VMEM((8 * SHARE, width), bf16),
            pltpu.VMEM((16, 8, SHARE), jnp.int32),
            pltpu.VMEM((8 * SHARE, 16 * SHARE), bf16),
            pltpu.VMEM((16 * SHARE, width), f32),
            pltpu.VMEM((8 * SHARE, width), f32),
            pltpu.VMEM((8, SHARE, width), f32),
            pltpu.VMEM((2 * MESSAGES, HALF, width), jnp.int16),
            pltpu.VMEM((2 * MESSAGES, HALF, width), jnp.int16),
            pltpu.VMEM((2 * MESSAGES, 8, 128), f32),
            pltpu.VMEM((2 * MESSAGES, 8, 128), f32),
            pltpu.SemaphoreType.DMA((2,)),
            pltpu.SemaphoreType.DMA((COPIES,)),
            pltpu.SemaphoreType.DMA((COPIES,)),
        ],
        compiler_params=pltpu.CompilerParams(
            collective_id=0, has_side_effects=True, vmem_limit_bytes=60 * 2**20
        ),
        cost_estimate=pl.CostEstimate(
            flops=6 * 2048 * 1024 * width, bytes_accessed=6 * SHARE * width * 2, transcendentals=2048 * 1024
        ),
        name="pair_loss_backward",
    )(sharpness_parameter, additive_intercept, picture_vectors, caption_vectors, matching_caption[None, :])
    scale = 0.5 * sharpness_parameter[0]
    return scale * picture_sums, scale * caption_sums


def solution(mesh):
    placed = (P(("blk", "grp"), None), P(("blk", "grp"), None), P(("blk", "grp")), P(), P())
    return jax.shard_map(
        per_device,
        mesh=mesh,
        in_specs=placed,
        out_specs=(P(("blk", "grp"), None), P(("blk", "grp"), None)),
        check_vma=False,
    )
```

time: 301 us -> 84.2 us (0.28)
  waiting for transfers between devices: 195 us -> 0 us
  Pallas kernels: 0 us -> 79.8 us
  matrix products: 48.8 us -> 0 us
  blocking collectives: 32.2 us -> 0 us
  between operations: 15.4 us -> 1.93 us
  local copies, waits for them, and re-layouts: 3.46 us -> 0 us
    reduce_scatter x2 -> x0, waiting for transfers between devices: 147 us -> none  [the longest x1 108 us: per_device(): lax.psum_scatter(image_total, 'grp', scatter_dimension=0, tiled=True)]
    pallas_call x0 -> x1, Pallas kernels: none -> 79.8 us  [per_device(): pl.pallas_call(kernel, out_shape=(out, out), in_specs=[smem, smem, anywhe...]
    dot_general x24 -> x0, matrix products: 48.8 us -> none  [the longest x8 18.2 us: rotation_step(): lax.dot_general(cohort_pictures, guest_captions, (((1,), (1,)), ((), ()))...]
    ppermute x7 -> x0, waiting for transfers between devices: 46.5 us -> none  [passed_along(): return lax.ppermute(block, axis, route)]
    all_gather x1 -> x0, blocking collectives: 32.2 us -> none  [per_device(): lax.all_gather(matching_caption, 'grp', axis=0, tiled=True)]
  transfers between devices with their start and end apart: 10 -> 0, of which waited for: 7 -> 0; matrix products, arithmetic and copies ran while one was open for 16% -> 0% of each run, Pallas kernels for 0% -> 0%
where the time goes in v1:
time: 84.2 us; the launch traced here: 84 us
  Pallas kernels  79.8 us (95%)
  other arithmetic  2.33 us (3%)
  between operations  1.93 us (2%)
    pallas_call x1, Pallas kernels, per_device(): pl.pallas_call(kernel, out_shape=(out, out), in_specs=[smem, smem, anywhe...  79.8 us
    mul x1, other arithmetic, per_device(): return (scale * picture_sums, scale * caption_sums)  2.33 us

profile of v1, /device:TPU:1, one launch (start us, length us, event | category | flops | bytes accessed | tf_op | source)
XLA Modules:
  0.0 84.0 jit_solution(17492132288271120186)
XLA Ops:
  1.9 79.8 %pair_loss_backward.1 = (f32[128,1152]{1,0:T(8,128)}, f32[128,1152]{1,0:T(8,128)}) custom-call(f32[1]{0:T(128)S(6)} %copy.7.sharp_ref, f32[1]{0:T(128)S(6)} %copy.8.shift_ref, bf16[128,1152]{1,0:T(8,128)(2,1)} %picture_ref.1, bf16[128,1152]{1,0:T(8,128)(2,1)} %caption_ref.1, s32[1,128]{1,0:T(1,128)} %bitcast.2), custom_call_target="tpu_custom_call" | custom-call | flops 14495514624 | bytes 1769472 | tf_op jit(solution)/shard_map/pair_loss_backward/pallas_call | solution.py:299
  81.7 2.3 %broadcast_multiply_fusion = (f32[128,1152]{1,0:T(8,128)}, f32[128,1152]{1,0:T(8,128)}) fusion(f32[128,1152]{1,0:T(8,128)} %get-tuple-element.5, f32[]{:T(128)} %bitcast, f32[128,1152]{1,0:T(8,128)} %get-tuple-element.4), kind=kLoop, calls=%fused_computation | loop fusion | flops 294912 | bytes 2359300 | tf_op jit(solution)/shard_map/mul | solution.py:329

commit v2 on v1

v2 whole, which is shorter than its diff:
```python
import functools

import jax
import jax.numpy as jnp
from jax import lax
from jax.experimental import pallas as pl
from jax.experimental.pallas import tpu as pltpu
from jax.sharding import PartitionSpec as P

MESH = pl.DeviceIdType.MESH
ORDER = [(0, 0), (3, 0), (1, 0), (0, 1), (2, 0), (3, 1), (1, 1), (2, 1)]
SLOT = {key: i for i, key in enumerate(ORDER)}
EARLY = 5
SHARE = 128
HALF = 64
UNIT = 32
TOP = 32767.0

ROUTE = {}
RESULT = {}
for part, at in (("A", 0), ("B", UNIT)):
    for step in range(4):
        ROUTE[f"x{step}{part}"] = ((step, 1), HALF + at, "pair", ())
    ROUTE["y" + part] = ((0, 1), at, "pair", ("Pc" + part, "Pd" + part))
    RESULT["oP" + part] = (at, ("pc" + part, "pd" + part, "y" + part))
    RESULT["oQ" + part] = (HALF + at, ("qc" + part, "qd" + part, "x0" + part))
    for tag, dx, low in (("P", 1, 0), ("p", 0, 0), ("q", 0, HALF)):
        came = lambda step: (f"x{step}{part}",) if tag == "q" else ()
        far, way = ("a", "plus") if part == "A" else ("b", "minus")
        ROUTE[tag + far] = ((2, dx), low + at, way, came(2))
        ROUTE[tag + "c" + part] = ((1, dx), low + at, "plus", came(1) + ((tag + "a",) if part == "A" else ()))
        ROUTE[tag + "d" + part] = ((3, dx), low + at, "minus", came(3) + ((tag + "b",) if part == "B" else ()))
NUMBER = {name: i for i, name in enumerate(ROUTE)}

PLAN = [
    "V3", "V7", "V4", "W7", "V1", "V2", "V5", "mp34", "V6", "mp76", "sh7", "sh4", "V0", "mc567", "tx2A",
    "ix2B", "tPcB", "iPa", "tPb", "tPdA", "tx1A", "tPa", "ix2A", "ipb", "tx2B", "sh6", "tx3A", "iPb", "mp5",
    "sh5", "tx3B", "ipa", "ix1B", "mc34", "iPcA", "tPdB", "tqa", "iPdA", "iqb", "tx0B", "ix3B", "tpb", "tPcA",
    "iqa", "ix3A", "tpa", "sh3", "mp12", "tqb", "sh1", "sh2", "tx1B", "iPdB", "ix1A", "ix0A", "tyB", "ix0B",
    "iPcB", "mc12", "tpdA", "tqcA", "tpdB", "iqdB", "iqcB", "tyA", "ipdB", "tpcB", "tqdA", "iqdA", "tqdB",
    "ipcB", "tpcA", "iyB", "iqcA", "ipcA", "ipdA", "mc0", "mp0", "sh0", "tqcB", "tx0A", "iyA", "toPB", "ioQB",
    "toPA", "ioPB", "ioQA", "toQB", "toQA", "ioPA",
]


def peers():
    b, g = lax.axis_index("blk"), lax.axis_index("grp")
    xl, y = b // 4, lax.rem(b, 4)
    z, low = g // 4, lax.rem(g, 4)
    xh, core = low // 2, lax.rem(low, 2)

    def at(xl, y, z, xh, core):
        return (xl * 4 + y, z * 4 + xh * 2 + core)

    up = lambda v: lax.rem(v + 1, 4)
    down = lambda v: lax.rem(v + 3, 4)
    pictures = (at(xl, y, up(z), xh, core), at(xl, y, down(z), xh, core), at(1 - xl, y, z, xh, core))
    captions = (at(xl, up(y), z, xh, core), at(xl, down(y), z, xh, core), at(1 - xl, y, z, 1 - xh, core))
    sibling = at(xl, y, z, xh, 1 - core)
    starts = []
    for dy, dx in ORDER:
        txl = 1 - xl if dx else xl
        txh = 1 - xh if dx else xh
        blk, grp = at(txl, lax.rem(y + dy, 4), z, txh, core)
        starts.append((blk * 16 + grp) * SHARE)
    return pictures, captions, sibling, starts


class Family:
    def __init__(self, shares, step, sums, other, devices, out, first):
        self.shares, self.step, self.sums, self.other = shares, step, sums, other
        self.plus, self.minus, self.pair = devices
        self.out, self.first = out, first
        self.sent = {}

    def rows(self, key, lo, hi):
        return self.shares.at[pl.ds(SLOT[key] * self.step + lo, hi - lo)]


def kernel(
    sharp_ref, shift_ref, picture_ref, caption_ref, label_ref, picture_out, caption_out,
    pictures, captions, labels, weights, picture_sums, caption_sums, sibling_sums,
    out_data, in_data, out_scale, in_scale, local_sem, send_sem, recv_sem,
):
    picture_peers, caption_peers, sibling, starts = peers()
    loads = [
        pltpu.make_async_copy(picture_ref, pictures.at[pl.ds(0, SHARE)], local_sem.at[0]),
        pltpu.make_async_copy(caption_ref, captions.at[pl.ds(0, SHARE)], local_sem.at[1]),
    ]
    for load in loads:
        load.start()
    barrier = pltpu.get_barrier_semaphore()
    everyone = [*picture_peers, *caption_peers, sibling]
    for device in everyone:
        pl.semaphore_signal(barrier, inc=1, device_id=device, device_id_type=MESH)
    labels[0] = jnp.broadcast_to(label_ref[...], (8, SHARE))
    half_sharp = sharp_ref[0] * 0.5
    half_shift = shift_ref[0] * 0.5
    for load in loads:
        load.wait()
    pl.semaphore_wait(barrier, len(everyone))

    width = picture_ref.shape[1]
    copies = []

    def send(src, dst, device):
        i = len(copies)
        copy = pltpu.make_async_remote_copy(
            src_ref=src, dst_ref=dst, send_sem=send_sem.at[i], recv_sem=recv_sem.at[i],
            device_id=device, device_id_type=MESH,
        )
        copy.start()
        copies.append(copy)
        return copy

    images = Family(pictures, 2 * SHARE, picture_sums, sibling_sums, picture_peers, picture_out, 0)
    texts = Family(captions, SHARE, caption_sums, None, caption_peers, caption_out, len(ROUTE))
    both = (images, texts)
    mid_p, mid_q = HALF // 2, HALF + HALF // 2

    def hop(f, name, key, lo, hi, to, device):
        f.sent[name] = send(f.rows(key, lo, hi), f.rows(to, lo, hi), device)

    def label_hop(name, key, to, device):
        images.sent[name] = send(labels.at[2 * SLOT[key]], labels.at[2 * SLOT[to]], device)

    def to_sibling(*keys):
        for key in keys:
            start = SLOT[key] * 2 * SHARE
            images.sent["s", key] = send(
                pictures.at[pl.ds(start, SHARE)], pictures.at[pl.ds(start + SHARE, SHARE)], sibling
            )
            images.sent["l", key] = send(labels.at[2 * SLOT[key]], labels.at[2 * SLOT[key] + 1], sibling)

    def arrive(f, *names):
        for name in names:
            f.sent[name].wait_recv()

    def from_sibling(*keys):
        for key in keys:
            arrive(images, ("s", key), ("l", key))

    def around(f, tag, key, to_plus, to_minus, lo):
        mid, hi = lo + HALF // 2, lo + HALF
        hop(f, tag + "+a", key, lo, mid, to_plus, f.plus)
        hop(f, tag + "-b", key, mid, hi, to_minus, f.minus)
        hop(f, tag + "+b", key, mid, hi, to_plus, f.plus)
        hop(f, tag + "-a", key, lo, mid, to_minus, f.minus)

    def onward(f, tag, dx, lo):
        arrive(f, tag + "+a", tag + "-b")
        hop(f, tag + "++", (3, dx), lo, lo + HALF // 2, (2, dx), f.plus)
        hop(f, tag + "--", (1, dx), lo + HALF // 2, lo + HALF, (2, dx), f.minus)

    to_sibling((0, 0))
    for f in both:
        around(f, "q", (0, 0), (3, 0), (1, 0), HALF)
        hop(f, "xp", (0, 0), 0, HALF, (0, 1), f.pair)
    label_hop("xl", (0, 0), (0, 1), images.pair)
    label_hop("l+", (0, 0), (3, 0), images.plus)
    label_hop("l-", (0, 0), (1, 0), images.minus)
    for f in both:
        around(f, "p", (0, 0), (3, 0), (1, 0), 0)
        hop(f, "xq", (0, 0), HALF, SHARE, (0, 1), f.pair)
    for f in both:
        onward(f, "q", 0, HALF)
    for f in both:
        arrive(f, "q+b", "q-a")
        hop(f, "xq1", (1, 0), HALF, SHARE, (1, 1), f.pair)
        hop(f, "xq3", (3, 0), HALF, SHARE, (3, 1), f.pair)
    arrive(images, "l+", "l-", "xl")
    label_hop("l++", (3, 0), (2, 0), images.plus)
    label_hop("L+", (0, 1), (3, 1), images.plus)
    label_hop("L-", (0, 1), (1, 1), images.minus)
    for f in both:
        onward(f, "p", 0, 0)
    for f in both:
        arrive(f, "xp")
        around(f, "P", (0, 1), (3, 1), (1, 1), 0)
    arrive(images, "p+b", "p-a")
    to_sibling((3, 0), (1, 0))
    arrive(images, "xq")
    to_sibling((0, 1))
    arrive(texts, "p+b", "p-a", "xq")
    arrive(images, "L+", "L-")
    label_hop("L++", (3, 1), (2, 1), images.plus)
    for f in both:
        arrive(f, "q++", "q--")
        hop(f, "xq2", (2, 0), HALF, SHARE, (2, 1), f.pair)

    def weigh(first_text, texts, first_image, images):
        @pl.loop(first_image, first_image + images)
        def _(ii):
            columns = pl.ds(pl.multiple_of(ii * 2 * SHARE, 2 * SHARE), 2 * SHARE)
            scores = lax.dot_general(
                captions[pl.ds(first_text * SHARE, texts * SHARE), :], pictures[columns, :],
                (((1,), (1,)), ((), ())), preferred_element_type=jnp.float32,
            )
            label = jnp.concatenate([labels[2 * ii, :1, :], labels[2 * ii + 1, :1, :]], axis=1)
            ids = lax.broadcasted_iota(jnp.int32, (SHARE, 2 * SHARE), 0)
            for j in range(texts):
                own = ids == label - starts[first_text + j]
                part = scores[j * SHARE : (j + 1) * SHARE] * half_sharp + half_shift
                twice = jnp.tanh(part) + jnp.where(own, -1.0, 1.0)
                weights[pl.ds((first_text + j) * SHARE, SHARE), columns] = twice.astype(jnp.bfloat16)

    def add(sums, rows, value, more):
        sums[rows, :] = sums[rows, :] + value if more else value

    def multiply_pictures(first, count, lo, hi, more=False):
        rows, inner = pl.ds(first * 2 * SHARE, count * 2 * SHARE), pl.ds(lo * SHARE, (hi - lo) * SHARE)
        value = lax.dot_general(
            weights[inner, rows], captions[inner, :], (((0,), (0,)), ((), ())), preferred_element_type=jnp.float32
        )
        add(picture_sums, rows, value, more)

    def multiply_captions(first, count, lo, hi, more=False):
        rows, inner = pl.ds(first * SHARE, count * SHARE), pl.ds(lo * 2 * SHARE, (hi - lo) * 2 * SHARE)
        value = jnp.dot(weights[rows, inner], pictures[inner, :], preferred_element_type=jnp.float32)
        add(caption_sums, rows, value, more)

    from_sibling((0, 0), (3, 0), (1, 0), (0, 1))
    for f in both:
        arrive(f, "p++", "p--")
    arrive(images, "l++")
    to_sibling((2, 0))
    weigh(0, EARLY, 0, 4)
    for f in both:
        onward(f, "P", 1, 0)
    from_sibling((2, 0))
    weigh(0, EARLY, 4, 1)
    multiply_captions(0, EARLY, 0, EARLY)
    for f in both:
        arrive(f, "P+b", "P-a", "xq1", "xq3")
    to_sibling((3, 1), (1, 1))
    multiply_pictures(0, EARLY, 0, EARLY)
    from_sibling((3, 1), (1, 1))
    arrive(images, "P++", "P--", "L++", "xq2")
    to_sibling((2, 1))
    weigh(0, EARLY, 5, 2)
    arrive(texts, "P++", "P--", "xq2")
    from_sibling((2, 1))

    def wide(tile):
        return jnp.concatenate([jnp.concatenate([tile] * (width // 128), axis=1)] * (UNIT // 8), axis=0)

    landed = set()

    def land(f, names):
        for name in names:
            if (f, name) not in landed:
                landed.add((f, name))
                for copy in f.sent[name]:
                    copy.wait_recv()

    def total(f, key, lo, names):
        x = f.sums[pl.ds(SLOT[key] * f.step + lo, UNIT), :]
        if f.other is not None:
            land(f, [f"sh{SLOT[key]}"])
            x = x + f.other[SLOT[key], pl.ds(lo, UNIT), :]
        land(f, names)
        for name in names:
            index = f.first + NUMBER[name]
            x = x + in_data[index].astype(jnp.int32).astype(jnp.float32) * wide(in_scale[index])
        return x

    def pass_on(f, name):
        key, lo, way, names = ROUTE[name]
        index = f.first + NUMBER[name]
        x = total(f, key, lo, names)
        size = jnp.abs(x)
        peak = jnp.full((8, 128), 1e-30, jnp.float32)
        for r in range(0, UNIT, 8):
            for c in range(0, width, 128):
                peak = jnp.maximum(peak, size[r : r + 8, c : c + 128])
        out_data[index] = jnp.round(x * wide(TOP / peak)).astype(jnp.int32).astype(jnp.int16)
        out_scale[index] = peak * (1.0 / TOP)
        device = getattr(f, way)
        f.sent[name] = (
            send(out_data.at[index], in_data.at[index], device),
            send(out_scale.at[index], in_scale.at[index], device),
        )

    def work(name):
        slots = [int(digit) for digit in name[2:] if digit.isdigit()]
        if name == "W7":
            weigh(0, EARLY, 7, 1)
        elif name[0] == "V":
            weigh(EARLY, 8 - EARLY, int(name[1]), 1)
        elif name[:2] in ("mp", "mc"):
            multiply = multiply_pictures if name[1] == "p" else multiply_captions
            begun = min(slots) < EARLY
            multiply(min(slots), len(slots), EARLY if begun else 0, 8, begun)
        elif name[:2] == "sh":
            i = slots[0]
            rows = pl.ds(i * 2 * SHARE + SHARE, SHARE)
            images.sent[name] = (send(picture_sums.at[rows], sibling_sums.at[i], sibling),)
        else:
            f = images if name[0] == "i" else texts
            if name[1:] in ROUTE:
                pass_on(f, name[1:])
            else:
                lo, names = RESULT[name[1:]]
                f.out[pl.ds(lo, UNIT), :] = total(f, (0, 0), lo, names)

    for name in PLAN:
        work(name)
    for copy in copies:
        copy.wait_send()


COPIES = 46 + 16 + 7 + 8 + 4 * len(ROUTE)


def per_device(picture_vectors, caption_vectors, matching_caption, sharpness_parameter, additive_intercept):
    width = picture_vectors.shape[1]
    f32, bf16 = jnp.float32, jnp.bfloat16
    out = jax.ShapeDtypeStruct((SHARE, width), f32)
    vmem, smem = pl.BlockSpec(memory_space=pltpu.VMEM), pl.BlockSpec(memory_space=pltpu.SMEM)
    anywhere = pl.BlockSpec(memory_space=pl.ANY)
    picture_sums, caption_sums = pl.pallas_call(
        kernel,
        out_shape=(out, out),
        in_specs=[smem, smem, anywhere, anywhere, vmem],
        out_specs=(vmem, vmem),
        scratch_shapes=[
            pltpu.VMEM((16 * SHARE, width), bf16),
            pltpu.VMEM((8 * SHARE, width), bf16),
            pltpu.VMEM((16, 8, SHARE), jnp.int32),
            pltpu.VMEM((8 * SHARE, 16 * SHARE), bf16),
            pltpu.VMEM((16 * SHARE, width), f32),
            pltpu.VMEM((8 * SHARE, width), f32),
            pltpu.VMEM((8, SHARE, width), f32),
            pltpu.VMEM((2 * len(ROUTE), UNIT, width), jnp.int16),
            pltpu.VMEM((2 * len(ROUTE), UNIT, width), jnp.int16),
            pltpu.VMEM((2 * len(ROUTE), 8, 128), f32),
            pltpu.VMEM((2 * len(ROUTE), 8, 128), f32),
            pltpu.SemaphoreType.DMA((2,)),
            pltpu.SemaphoreType.DMA((COPIES,)),
            pltpu.SemaphoreType.DMA((COPIES,)),
        ],
        compiler_params=pltpu.CompilerParams(
            collective_id=0, has_side_effects=True, vmem_limit_bytes=60 * 2**20
        ),
        cost_estimate=pl.CostEstimate(
            flops=6 * 2048 * 1024 * width, bytes_accessed=6 * SHARE * width * 2, transcendentals=2048 * 1024
        ),
        name="pair_loss_backward",
    )(sharpness_parameter, additive_intercept, picture_vectors, caption_vectors, matching_caption[None, :])
    scale = 0.5 * sharpness_parameter[0]
    return scale * picture_sums, scale * caption_sums


def solution(mesh):
    placed = (P(("blk", "grp"), None), P(("blk", "grp"), None), P(("blk", "grp")), P(), P())
    return jax.shard_map(
        per_device,
        mesh=mesh,
        in_specs=placed,
        out_specs=(P(("blk", "grp"), None), P(("blk", "grp"), None)),
        check_vma=False,
    )
```

time: 84.2 us -> 67.8 us (0.81)
  Pallas kernels: 79.8 us -> 63.4 us
    pallas_call x1, Pallas kernels: 79.8 us -> 63.4 us  [per_device(): pl.pallas_call(kernel, out_shape=(out, out), in_specs=[smem, smem, anywhe...]
where the time goes in v2:
time: 67.8 us; the launch traced here: 67.7 us
  Pallas kernels  63.4 us (94%)
  other arithmetic  2.33 us (3%)
  between operations  1.93 us (3%)
    pallas_call x1, Pallas kernels, per_device(): pl.pallas_call(kernel, out_shape=(out, out), in_specs=[smem, smem, anywhe...  63.4 us
    mul x1, other arithmetic, per_device(): return (scale * picture_sums, scale * caption_sums)  2.33 us

profile of v2, /device:TPU:1, one launch (start us, length us, event | category | flops | bytes accessed | tf_op | source)
XLA Modules:
  0.0 67.7 jit_solution(589718855416300228)
XLA Ops:
  1.9 63.4 %pair_loss_backward.1 = (f32[128,1152]{1,0:T(8,128)}, f32[128,1152]{1,0:T(8,128)}) custom-call(f32[1]{0:T(128)S(6)} %copy.7.sharp_ref, f32[1]{0:T(128)S(6)} %copy.8.shift_ref, bf16[128,1152]{1,0:T(8,128)(2,1)} %picture_ref.1, bf16[128,1152]{1,0:T(8,128)(2,1)} %caption_ref.1, s32[1,128]{1,0:T(1,128)} %bitcast.2), custom_call_target="tpu_custom_call" | custom-call | flops 14495514624 | bytes 1769472 | tf_op jit(solution)/shard_map/pair_loss_backward/pallas_call | solution.py:321
  65.3 2.3 %broadcast_multiply_fusion = (f32[128,1152]{1,0:T(8,128)}, f32[128,1152]{1,0:T(8,128)}) fusion(f32[128,1152]{1,0:T(8,128)} %get-tuple-element.5, f32[]{:T(128)} %bitcast, f32[128,1152]{1,0:T(8,128)} %get-tuple-element.4), kind=kLoop, calls=%fused_computation | loop fusion | flops 294912 | bytes 2359300 | tf_op jit(solution)/shard_map/mul | solution.py:351

commit v3 on v2

--- a/solution.py
+++ b/solution.py
@@ -14,7 +14,8 @@
 SHARE = 128
 HALF = 64
 UNIT = 32
-TOP = 32767.0
+TILES = 9
+TOP = 32760.0
 
 ROUTE = {}
 RESULT = {}
@@ -33,13 +34,14 @@
 NUMBER = {name: i for i, name in enumerate(ROUTE)}
 
 PLAN = [
-    "V3", "V7", "V4", "W7", "V1", "V2", "V5", "mp34", "V6", "mp76", "sh7", "sh4", "V0", "mc567", "tx2A",
-    "ix2B", "tPcB", "iPa", "tPb", "tPdA", "tx1A", "tPa", "ix2A", "ipb", "tx2B", "sh6", "tx3A", "iPb", "mp5",
-    "sh5", "tx3B", "ipa", "ix1B", "mc34", "iPcA", "tPdB", "tqa", "iPdA", "iqb", "tx0B", "ix3B", "tpb", "tPcA",
-    "iqa", "ix3A", "tpa", "sh3", "mp12", "tqb", "sh1", "sh2", "tx1B", "iPdB", "ix1A", "ix0A", "tyB", "ix0B",
-    "iPcB", "mc12", "tpdA", "tqcA", "tpdB", "iqdB", "iqcB", "tyA", "ipdB", "tpcB", "tqdA", "iqdA", "tqdB",
-    "ipcB", "tpcA", "iyB", "iqcA", "ipcA", "ipdA", "mc0", "mp0", "sh0", "tqcB", "tx0A", "iyA", "toPB", "ioQB",
-    "toPA", "ioPB", "ioQA", "toQB", "toQA", "ioPA",
+    "V4", "V2", "V7", "V6", "W7", "mp76", "sh6p", "sh7q", "V5", "sh7p", "mc12", "tpdA", "iPcB", "mc34",
+    "tx0B", "ix2A", "V1", "iPb", "iPa", "tx0A", "mp5", "sh5p", "sh5q", "ix2B", "sh6q", "tpb", "tpcB", "V3",
+    "V0", "mc7", "tx2A", "tPa", "tPb", "ix3A", "tx2B", "iPdA", "ix1A", "ix1B", "mp12", "sh2q", "sh1q", "sh1p",
+    "mp4", "sh4q", "sh4p", "iPcA", "tpdB", "tpa", "iPdB", "ix3B", "mc56", "tx3B", "tPcB", "tPdA", "ipdA",
+    "tPcA", "tx3A", "iqa", "iqdA", "iqb", "tqa", "tx1B", "mc0", "ipb", "ipa", "sh2p", "mp3", "sh3q", "tPdB",
+    "mp0", "tqb", "tpcA", "ipcB", "sh0q", "sh0p", "sh3p", "tx1A", "ix0A", "ix0B", "iqcB", "iqcA", "iyB",
+    "iyA", "tyB", "tqdA", "tyA", "ipcA", "tqdB", "tqcB", "iqdB", "tqcA", "ipdB", "toPB", "toQB", "ioQA",
+    "ioQB", "toPA", "toQA", "ioPB", "ioPA",
 ]
 
 
@@ -79,13 +81,14 @@
 
 def kernel(
     sharp_ref, shift_ref, picture_ref, caption_ref, label_ref, picture_out, caption_out,
-    pictures, captions, labels, weights, picture_sums, caption_sums, sibling_sums,
-    out_data, in_data, out_scale, in_scale, local_sem, send_sem, recv_sem,
+    pictures, captions, own_labels, labels, weights, picture_sums, caption_sums, sibling_sums,
+    out_data, in_data, local_sem, send_sem, recv_sem,
 ):
     picture_peers, caption_peers, sibling, starts = peers()
     loads = [
         pltpu.make_async_copy(picture_ref, pictures.at[pl.ds(0, SHARE)], local_sem.at[0]),
         pltpu.make_async_copy(caption_ref, captions.at[pl.ds(0, SHARE)], local_sem.at[1]),
+        pltpu.make_async_copy(label_ref, own_labels, local_sem.at[2]),
     ]
     for load in loads:
         load.start()
@@ -93,11 +96,11 @@
     everyone = [*picture_peers, *caption_peers, sibling]
     for device in everyone:
         pl.semaphore_signal(barrier, inc=1, device_id=device, device_id_type=MESH)
-    labels[0] = jnp.broadcast_to(label_ref[...], (8, SHARE))
     half_sharp = sharp_ref[0] * 0.5
     half_shift = shift_ref[0] * 0.5
     for load in loads:
         load.wait()
+    labels[0] = jnp.broadcast_to(own_labels[...], (8, SHARE))
     pl.semaphore_wait(barrier, len(everyone))
 
     width = picture_ref.shape[1]
@@ -224,9 +227,10 @@
         arrive(f, "p++", "p--")
     arrive(images, "l++")
     to_sibling((2, 0))
-    weigh(0, EARLY, 0, 4)
+    weigh(0, EARLY, 0, 2)
     for f in both:
         onward(f, "P", 1, 0)
+    weigh(0, EARLY, 2, 2)
     from_sibling((2, 0))
     weigh(0, EARLY, 4, 1)
     multiply_captions(0, EARLY, 0, EARLY)
@@ -256,12 +260,15 @@
     def total(f, key, lo, names):
         x = f.sums[pl.ds(SLOT[key] * f.step + lo, UNIT), :]
         if f.other is not None:
-            land(f, [f"sh{SLOT[key]}"])
+            land(f, [f"sh{SLOT[key]}" + "pq"[lo // HALF]])
             x = x + f.other[SLOT[key], pl.ds(lo, UNIT), :]
         land(f, names)
         for name in names:
             index = f.first + NUMBER[name]
-            x = x + in_data[index].astype(jnp.int32).astype(jnp.float32) * wide(in_scale[index])
+            rows = [jnp.concatenate([in_data[index, TILES * r + c] for c in range(TILES)], axis=1) for r in (0, 1)]
+            power = in_data[index, 2 * TILES].astype(jnp.int32).astype(jnp.float32)
+            scale = jnp.exp2(power[:8]) * (1.0 / TOP)
+            x = x + jnp.concatenate(rows, axis=0).astype(jnp.int32).astype(jnp.float32) * wide(scale)
         return x
 
     def pass_on(f, name):
@@ -273,13 +280,20 @@
         for r in range(0, UNIT, 8):
             for c in range(0, width, 128):
                 peak = jnp.maximum(peak, size[r : r + 8, c : c + 128])
-        out_data[index] = jnp.round(x * wide(TOP / peak)).astype(jnp.int32).astype(jnp.int16)
-        out_scale[index] = peak * (1.0 / TOP)
-        device = getattr(f, way)
-        f.sent[name] = (
-            send(out_data.at[index], in_data.at[index], device),
-            send(out_scale.at[index], in_scale.at[index], device),
-        )
+        power = jnp.ceil(jnp.log2(peak))
+        whole = jnp.round(x * wide(TOP * jnp.exp2(-power))).astype(jnp.int32).astype(jnp.int16)
+        for r in (0, 1):
+            for c in range(TILES):
+                out_data[index, TILES * r + c] = whole[16 * r : 16 * r + 16, 128 * c : 128 * c + 128]
+        out_data[index, 2 * TILES] = jnp.concatenate([power, power], axis=0).astype(jnp.int32).astype(jnp.int16)
+        f.sent[name] = (send(out_data.at[index], in_data.at[index], getattr(f, way)),)
+
+    drained = [0]
+
+    def drain(keep):
+        while drained[0] < len(copies) - keep:
+            copies[drained[0]].wait_send()
+            drained[0] += 1
 
     def work(name):
         slots = [int(digit) for digit in name[2:] if digit.isdigit()]
@@ -293,23 +307,24 @@
             multiply(min(slots), len(slots), EARLY if begun else 0, 8, begun)
         elif name[:2] == "sh":
             i = slots[0]
-            rows = pl.ds(i * 2 * SHARE + SHARE, SHARE)
-            images.sent[name] = (send(picture_sums.at[rows], sibling_sums.at[i], sibling),)
+            at = HALF if name[-1] == "q" else 0
+            rows = pl.ds(i * 2 * SHARE + SHARE + at, HALF)
+            images.sent[name] = (send(picture_sums.at[rows], sibling_sums.at[i, pl.ds(at, HALF)], sibling),)
         else:
             f = images if name[0] == "i" else texts
             if name[1:] in ROUTE:
                 pass_on(f, name[1:])
             else:
                 lo, names = RESULT[name[1:]]
+                drain(24)
                 f.out[pl.ds(lo, UNIT), :] = total(f, (0, 0), lo, names)
 
     for name in PLAN:
         work(name)
-    for copy in copies:
-        copy.wait_send()
-
-
-COPIES = 46 + 16 + 7 + 8 + 4 * len(ROUTE)
+    drain(0)
+
+
+COPIES = 46 + 16 + 7 + 16 + 2 * len(ROUTE)
 
 
 def per_device(picture_vectors, caption_vectors, matching_caption, sharpness_parameter, additive_intercept):
@@ -317,36 +332,39 @@
     f32, bf16 = jnp.float32, jnp.bfloat16
     out = jax.ShapeDtypeStruct((SHARE, width), f32)
     vmem, smem = pl.BlockSpec(memory_space=pltpu.VMEM), pl.BlockSpec(memory_space=pltpu.SMEM)
-    anywhere = pl.BlockSpec(memory_space=pl.ANY)
+    anywhere = pl.BlockSpec(memory_space=pltpu.HBM)
+    arrays = [
+        pltpu.with_memory_space_constraint(array, pltpu.HBM)
+        for array in (picture_vectors, caption_vectors, matching_caption[None, :])
+    ]
     picture_sums, caption_sums = pl.pallas_call(
         kernel,
         out_shape=(out, out),
-        in_specs=[smem, smem, anywhere, anywhere, vmem],
+        in_specs=[smem, smem, anywhere, anywhere, anywhere],
         out_specs=(vmem, vmem),
         scratch_shapes=[
             pltpu.VMEM((16 * SHARE, width), bf16),
             pltpu.VMEM((8 * SHARE, width), bf16),
+            pltpu.VMEM((1, SHARE), jnp.int32),
             pltpu.VMEM((16, 8, SHARE), jnp.int32),
             pltpu.VMEM((8 * SHARE, 16 * SHARE), bf16),
             pltpu.VMEM((16 * SHARE, width), f32),
             pltpu.VMEM((8 * SHARE, width), f32),
             pltpu.VMEM((8, SHARE, width), f32),
-            pltpu.VMEM((2 * len(ROUTE), UNIT, width), jnp.int16),
-            pltpu.VMEM((2 * len(ROUTE), UNIT, width), jnp.int16),
-            pltpu.VMEM((2 * len(ROUTE), 8, 128), f32),
-            pltpu.VMEM((2 * len(ROUTE), 8, 128), f32),
-            pltpu.SemaphoreType.DMA((2,)),
+            pltpu.VMEM((2 * len(ROUTE), 2 * TILES + 1, 16, 128), jnp.int16),
+            pltpu.VMEM((2 * len(ROUTE), 2 * TILES + 1, 16, 128), jnp.int16),
+            pltpu.SemaphoreType.DMA((3,)),
             pltpu.SemaphoreType.DMA((COPIES,)),
             pltpu.SemaphoreType.DMA((COPIES,)),
         ],
         compiler_params=pltpu.CompilerParams(
-            collective_id=0, has_side_effects=True, vmem_limit_bytes=60 * 2**20
+            collective_id=0, has_side_effects=True, vmem_limit_bytes=46 * 2**20
         ),
         cost_estimate=pl.CostEstimate(
             flops=6 * 2048 * 1024 * width, bytes_accessed=6 * SHARE * width * 2, transcendentals=2048 * 1024
         ),
         name="pair_loss_backward",
-    )(sharpness_parameter, additive_intercept, picture_vectors, caption_vectors, matching_caption[None, :])
+    )(sharpness_parameter, additive_intercept, *arrays)
     scale = 0.5 * sharpness_parameter[0]
     return scale * picture_sums, scale * caption_sums
 

time: 67.8 us -> 63.1 us (0.931)
  Pallas kernels: 63.4 us -> 59.4 us
  other arithmetic: 2.33 us -> 1.09 us
    pallas_call x1, Pallas kernels: 63.4 us -> 59.4 us  [per_device(): pl.pallas_call(kernel, out_shape=(out, out), in_specs=[smem, smem, anywhe...]
    mul x1, other arithmetic: 2.33 us -> 1.09 us  [per_device(): return (scale * picture_sums, scale * caption_sums)]
where the time goes in v3:
time: 63.1 us; the launch traced here: 62.5 us
  Pallas kernels  59.4 us (94%)
  between operations  1.93 us (3%)
  other arithmetic  1.09 us (2%)
    pallas_call x1, Pallas kernels, per_device(): pl.pallas_call(kernel, out_shape=(out, out), in_specs=[smem, smem, anywhe...  59.4 us

profile of v3, /device:TPU:1, one launch (start us, length us, event | category | flops | bytes accessed | tf_op | source)
XLA Modules:
  0.0 62.5 jit_solution(6701396826463996761)
XLA Ops:
  1.9 59.4 %pair_loss_backward.1 = (f32[128,1152]{1,0:T(8,128)S(1)}, f32[128,1152]{1,0:T(8,128)S(1)}) custom-call(f32[1]{0:T(128)S(6)} %copy.7.sharp_ref, f32[1]{0:T(128)S(6)} %copy.8.shift_ref, bf16[128,1152]{1,0:T(8,128)(2,1)} %picture_ref.1, bf16[128,1152]{1,0:T(8,128)(2,1)} %caption_ref.1, s32[1,128]{1,0:T(1,128)} %bitcast.2), custom_call_target="tpu_custom_call" | custom-call | flops 14495514624 | bytes 1769472 | tf_op jit(solution)/shard_map/pair_loss_backward/pallas_call | solution.py:340
  61.4 1.1 %broadcast_multiply_fusion = (f32[128,1152]{1,0:T(8,128)}, f32[128,1152]{1,0:T(8,128)}) fusion(f32[128,1152]{1,0:T(8,128)S(1)} %get-tuple-element.5, f32[]{:T(128)} %bitcast, f32[128,1152]{1,0:T(8,128)S(1)} %get-tuple-element.4), kind=kLoop, calls=%fused_computation | loop fusion | flops 294912 | bytes 2359300 | tf_op jit(solution)/shard_map/mul | solution.py:369

commit v4 on v3

--- a/solution.py
+++ b/solution.py
@@ -34,14 +34,14 @@
 NUMBER = {name: i for i, name in enumerate(ROUTE)}
 
 PLAN = [
-    "V4", "V2", "V7", "V6", "W7", "mp76", "sh6p", "sh7q", "V5", "sh7p", "mc12", "tpdA", "iPcB", "mc34",
-    "tx0B", "ix2A", "V1", "iPb", "iPa", "tx0A", "mp5", "sh5p", "sh5q", "ix2B", "sh6q", "tpb", "tpcB", "V3",
-    "V0", "mc7", "tx2A", "tPa", "tPb", "ix3A", "tx2B", "iPdA", "ix1A", "ix1B", "mp12", "sh2q", "sh1q", "sh1p",
-    "mp4", "sh4q", "sh4p", "iPcA", "tpdB", "tpa", "iPdB", "ix3B", "mc56", "tx3B", "tPcB", "tPdA", "ipdA",
-    "tPcA", "tx3A", "iqa", "iqdA", "iqb", "tqa", "tx1B", "mc0", "ipb", "ipa", "sh2p", "mp3", "sh3q", "tPdB",
-    "mp0", "tqb", "tpcA", "ipcB", "sh0q", "sh0p", "sh3p", "tx1A", "ix0A", "ix0B", "iqcB", "iqcA", "iyB",
-    "iyA", "tyB", "tqdA", "tyA", "ipcA", "tqdB", "tqcB", "iqdB", "tqcA", "ipdB", "toPB", "toQB", "ioQA",
-    "ioQB", "toPA", "toQA", "ioPB", "ioPA",
+    "V4", "V1", "W7", "V0", "V6", "V3", "V7", "mp76", "sh7q", "sh7p", "sh6p", "sh6q", "mc34", "tx0B", "tpa",
+    "mp1", "iPb", "iPa", "ix2B", "sh1p", "ix2A", "mp4", "sh4p", "iPcB", "ix1B", "sh4q", "tx0A", "tpb", "V2",
+    "ipdA", "V5", "ipa", "mc7", "tPa", "tx2A", "tPb", "ipb", "mp5", "sh5q", "tx2B", "ix1A", "sh5p", "mc12",
+    "tpcB", "tpdB", "tpcA", "mc56", "tPdA", "iqa", "tx3A", "iPdB", "tPcA", "tPdB", "tqa", "tx3B", "ix3A",
+    "ix3B", "ipdB", "tx1A", "tx1B", "tPcB", "iPcA", "iPdA", "mp3", "sh3q", "mp2", "sh2q", "tqb", "sh3p",
+    "sh1q", "tpdA", "mp0", "ix0B", "ix0A", "iqcA", "iqcB", "sh0q", "iqb", "sh2p", "mc0", "sh0p", "tqdA",
+    "iyB", "iqdA", "tyA", "ipcB", "ipcA", "iyA", "tqcA", "tqdB", "iqdB", "tyB", "tqcB", "ioQA", "toPA",
+    "toQA", "ioPB", "ioQB", "toPB", "toQB", "ioPA",
 ]
 
 
@@ -233,11 +233,10 @@
     weigh(0, EARLY, 2, 2)
     from_sibling((2, 0))
     weigh(0, EARLY, 4, 1)
-    multiply_captions(0, EARLY, 0, EARLY)
     for f in both:
         arrive(f, "P+b", "P-a", "xq1", "xq3")
     to_sibling((3, 1), (1, 1))
-    multiply_pictures(0, EARLY, 0, EARLY)
+    multiply_captions(0, EARLY, 0, EARLY)
     from_sibling((3, 1), (1, 1))
     arrive(images, "P++", "P--", "L++", "xq2")
     to_sibling((2, 1))
@@ -303,7 +302,7 @@
             weigh(EARLY, 8 - EARLY, int(name[1]), 1)
         elif name[:2] in ("mp", "mc"):
             multiply = multiply_pictures if name[1] == "p" else multiply_captions
-            begun = min(slots) < EARLY
+            begun = name[1] == "c" and min(slots) < EARLY
             multiply(min(slots), len(slots), EARLY if begun else 0, 8, begun)
         elif name[:2] == "sh":
             i = slots[0]

time: 63.1 us -> 61.4 us (0.973)
  Pallas kernels: 59.4 us -> 58.2 us
    pallas_call x1, Pallas kernels: 59.4 us -> 58.2 us  [per_device(): pl.pallas_call(kernel, out_shape=(out, out), in_specs=[smem, smem, anywhe...]
where the time goes in v4:
time: 61.4 us; the launch traced here: 61.3 us
  Pallas kernels  58.2 us (95%)
  between operations  1.93 us (3%)
  other arithmetic  1.09 us (2%)
    pallas_call x1, Pallas kernels, per_device(): pl.pallas_call(kernel, out_shape=(out, out), in_specs=[smem, smem, anywhe...  58.2 us

profile of v4, /device:TPU:1, one launch (start us, length us, event | category | flops | bytes accessed | tf_op | source)
XLA Modules:
  0.0 61.3 jit_solution(2482289903564027889)
XLA Ops:
  1.9 58.2 %pair_loss_backward.1 = (f32[128,1152]{1,0:T(8,128)S(1)}, f32[128,1152]{1,0:T(8,128)S(1)}) custom-call(f32[1]{0:T(128)S(6)} %copy.7.sharp_ref, f32[1]{0:T(128)S(6)} %copy.8.shift_ref, bf16[128,1152]{1,0:T(8,128)(2,1)} %picture_ref.1, bf16[128,1152]{1,0:T(8,128)(2,1)} %caption_ref.1, s32[1,128]{1,0:T(1,128)} %bitcast.2), custom_call_target="tpu_custom_call" | custom-call | flops 14495514624 | bytes 1769472 | tf_op jit(solution)/shard_map/pair_loss_backward/pallas_call | solution.py:339
  60.2 1.1 %broadcast_multiply_fusion = (f32[128,1152]{1,0:T(8,128)}, f32[128,1152]{1,0:T(8,128)}) fusion(f32[128,1152]{1,0:T(8,128)S(1)} %get-tuple-element.5, f32[]{:T(128)} %bitcast, f32[128,1152]{1,0:T(8,128)S(1)} %get-tuple-element.4), kind=kLoop, calls=%fused_computation | loop fusion | flops 294912 | bytes 2359300 | tf_op jit(solution)/shard_map/mul | solution.py:368

commit v5 on v4

--- a/solution.py
+++ b/solution.py
@@ -270,8 +270,17 @@
             x = x + jnp.concatenate(rows, axis=0).astype(jnp.int32).astype(jnp.float32) * wide(scale)
         return x
 
+    drained = [0]
+
+    def drain(keep):
+        while drained[0] < len(copies) - keep:
+            copies[drained[0]].wait_send()
+            drained[0] += 1
+
     def pass_on(f, name):
         key, lo, way, names = ROUTE[name]
+        if name[0] == "y":
+            drain(40)
         index = f.first + NUMBER[name]
         x = total(f, key, lo, names)
         size = jnp.abs(x)
@@ -286,13 +295,6 @@
                 out_data[index, TILES * r + c] = whole[16 * r : 16 * r + 16, 128 * c : 128 * c + 128]
         out_data[index, 2 * TILES] = jnp.concatenate([power, power], axis=0).astype(jnp.int32).astype(jnp.int16)
         f.sent[name] = (send(out_data.at[index], in_data.at[index], getattr(f, way)),)
-
-    drained = [0]
-
-    def drain(keep):
-        while drained[0] < len(copies) - keep:
-            copies[drained[0]].wait_send()
-            drained[0] += 1
 
     def work(name):
         slots = [int(digit) for digit in name[2:] if digit.isdigit()]

time: 61.4 us -> 61.4 us (level)
  no operation moved by 1% of the time
where the time goes in v5:
time: 61.4 us; the launch traced here: 61.3 us
  Pallas kernels  58.2 us (95%)
  between operations  1.93 us (3%)
  other arithmetic  1.09 us (2%)
    pallas_call x1, Pallas kernels, per_device(): pl.pallas_call(kernel, out_shape=(out, out), in_specs=[smem, smem, anywhe...  58.2 us

profile of v5, /device:TPU:1, one launch (start us, length us, event | category | flops | bytes accessed | tf_op | source)
XLA Modules:
  0.0 61.3 jit_solution(6490605211068418446)
XLA Ops:
  1.9 58.2 %pair_loss_backward.1 = (f32[128,1152]{1,0:T(8,128)S(1)}, f32[128,1152]{1,0:T(8,128)S(1)}) custom-call(f32[1]{0:T(128)S(6)} %copy.7.sharp_ref, f32[1]{0:T(128)S(6)} %copy.8.shift_ref, bf16[128,1152]{1,0:T(8,128)(2,1)} %picture_ref.1, bf16[128,1152]{1,0:T(8,128)(2,1)} %caption_ref.1, s32[1,128]{1,0:T(1,128)} %bitcast.2), custom_call_target="tpu_custom_call" | custom-call | flops 14495514624 | bytes 1769472 | tf_op jit(solution)/shard_map/pair_loss_backward/pallas_call | solution.py:341
  60.2 1.1 %broadcast_multiply_fusion = (f32[128,1152]{1,0:T(8,128)}, f32[128,1152]{1,0:T(8,128)}) fusion(f32[128,1152]{1,0:T(8,128)S(1)} %get-tuple-element.5, f32[]{:T(128)} %bitcast, f32[128,1152]{1,0:T(8,128)S(1)} %get-tuple-element.4), kind=kLoop, calls=%fused_computation | loop fusion | flops 294912 | bytes 2359300 | tf_op jit(solution)/shard_map/mul | solution.py:370
